TPU v7x, 256 devices: a whole 4x4x8 slice. The times are simulated.
256 devices in a mesh: cd: 32 (over x, y, core), ab: 8 (over z).
Axes of the slice: x: 4, y: 4, z: 8, core: 2. Of those that a mesh axis runs over, the one named last changes fastest.
Arguments:
- amplitudes: float32 [1024, 65536], P('ab', 'cd'), may hold values from -6 to 6
- integrals: float32 [65536, 4096], P('cd', 'ab'), may hold values from -0.0234375 to 0.0234375
- live_tiles: int32 [256], P('cd'), may hold values from 0 to 1, as said below
- residual_in: float32 [1024, 4096], P(('ab', 'cd')), may hold values from -6 to 6
Outputs:
- residual_out: float32 [1024, 4096], P(('ab', 'cd'))
Inputs may be any that keep to these rules, and one draw needn't show every extreme that they name: live_tiles[t] is 1 where tile t of 256 contracted pairs carries integrals and 0 where it is screened out; the 8 tiles of each index of cd hold at least one live tile.
All inputs are finite; a program needn't handle non-finite values.
Results may differ from a plain program's by a relative error of at most 0.0001.
Values sent between devices are 32-bit elements; how exact they have to be, the bound alone decides.
A program may use at most 128 MiB of HBM per device.

v0:
```python
import jax
import jax.numpy as jnp
from jax import lax
from jax.sharding import PartitionSpec as P

TILE = 256


def dense_product(left_part, right_part, live_tiles, tile_size):
    weights = jnp.repeat(
        live_tiles.astype(jnp.float32), tile_size, total_repeat_length=right_part.shape[0]
    )
    return jnp.dot(
        left_part,
        right_part * weights[:, None],
        preferred_element_type=jnp.float32,
        precision=lax.Precision.HIGHEST,
    )


def per_device(amplitudes, integrals, live_tiles, residual_in):
    tile_size = TILE
    count_ab = lax.axis_size("ab")
    count_cd = lax.axis_size("cd")
    out_rows = residual_in.shape[0]
    partial_sum = dense_product(
        lax.all_gather(amplitudes, "ab", axis=0, tiled=True), integrals, live_tiles, tile_size
    )
    columns_dev = partial_sum.shape[1]
    ordered = partial_sum.reshape(count_ab, count_cd, out_rows, columns_dev).transpose(1, 0, 2, 3)
    ordered = ordered.reshape(count_cd * count_ab * out_rows, columns_dev)
    reduced = lax.psum_scatter(ordered, "cd", scatter_dimension=0, tiled=True)
    placed = lax.all_to_all(
        reduced.reshape(count_ab, out_rows, columns_dev),
        "ab",
        split_axis=0,
        concat_axis=2,
        tiled=True,
    )
    ladder = placed.reshape(out_rows, count_ab * columns_dev)
    return residual_in + ladder


def solution(mesh):
    return jax.shard_map(
        per_device,
        mesh=mesh,
        in_specs=(P("ab", "cd"), P("cd", "ab"), P("cd"), P(("ab", "cd"), None)),
        out_specs=P(("ab", "cd"), None),
        check_vma=False,
    )
```

profile of v0, /device:TPU:1, one launch (start us, length us, event | category | flops | bytes accessed | tf_op | source)
XLA Modules:
  0.0 251.9 jit_solution(15522301821664691959)
XLA Ops:
  6.5 0.0 all-gather.2.cloned.1.call-start
  6.5 0.7 all-gather.2.cloned.1.call-update
  7.3 0.0 reduce-scatter.2.cloned.1.call-start
  7.3 0.7 convert_element_type.3
  8.0 0.7 fusion.6
  8.6 5.9 %select_select_fusion = f32[2048]{0:T(1024)S(1)} fusion(pred[2048]{0:T(1024)(128)(4,1)} %constant.109, pred[2048]{0:T(1024)(128)(4,1)} %constant.110, pred[2048]{0:T(1024)(128)(4,1)} %constant.111, pred[2048]{0:T(1024)(128)(4,1)} %constant.112, pred[2048]{0:T(1024)(128)(4,1)} %constant.113, pred[2048]{0:T(1024)(128)(4,1)} %constant.114, ...), kind=kLoop, calls=%fused_computation.4 | loop fusion | flops 14336 | bytes 22560 | tf_op jit(solution)/shard_map/jit(_take)/gather | solution.py:10
  14.5 92.7 %all-gather.2.cloned.1.call-done = f32[1024,2048]{1,0:T(8,128)} async-done(((f32[128,2048]{1,0:T(8,128)}), f32[1024,2048]{1,0:T(8,128)}) %all-gather.2.cloned.1.call-update) | async-done | bytes 8388624 | tf_op jit(solution)/shard_map/all_gather | solution.py:27
  107.1 31.5 %fusion.3 = f32[1024,512]{0,1:T(8,128)} fusion(f32[1024,2048]{1,0:T(8,128)} %all-gather.2.cloned.1.call-done, f32[2048,512]{1,0:T(8,128)} %param.7, f32[2048]{0:T(1024)S(1)} %select_select_fusion), kind=kOutput, calls=%fused_computation.3 | convolution fusion | flops 12885950464 | bytes 14688256 | tf_op jit(solution)/shard_map/dot_general | solution.py:13
  138.6 1.9 copy.5
  140.6 1.7 reshape.95
  142.2 2.2 copy.6
  144.4 0.0 copy-start
  144.4 1.8 reshape.96
  146.2 0.0 reduce-scatter.2.cloned.1.call-update
  146.2 83.6 %reduce-scatter.2.cloned.1.call-done = f32[32,512]{1,0:T(8,128)} async-done(((f32[1024,512]{1,0:T(8,128)}), f32[32,512]{1,0:T(8,128)}) %reduce-scatter.2.cloned.1.call-update) | async-done | bytes 65552 | tf_op jit(solution)/shard_map/reduce_scatter | solution.py:32
  229.8 0.9 reshape.97
  230.7 13.8 %all_to_all.15 = f32[8,4,512]{2,1,0:T(4,128)S(1)} all-to-all(f32[8,4,512]{2,1,0:T(4,128)S(1)} %reshape.97), channel_id=1, replica_groups=mesh['cd'=32,'ab'=8] {'ab'}, dimensions={0} | all-to-all | bytes 131072 | tf_op jit(solution)/shard_map/all_to_all | solution.py:33
  244.4 0.0 copy-done
  244.4 0.6 add.42
Async XLA Ops:
  6.5 100.6 %all-gather.2.cloned.1.call-start = ((), (), s32[]{:S(2)}) async-start(), calls=%async_computation.2 | async-start | bytes 9437184 | tf_op jit(solution)/shard_map/all_gather | solution.py:27
  7.3 222.6 %reduce-scatter.2.cloned.1.call-start = ((), (), s32[]{:S(2)}) async-start(), calls=%async_computation.3 | async-start | bytes 2162688 | tf_op jit(solution)/shard_map/reduce_scatter | solution.py:32
  144.4 100.0 %copy-start = (f32[4,4096]{1,0:T(4,128)S(1)}, f32[4,4096]{1,0:T(4,128)}, u32[]{:S(2)}) copy-start(f32[4,4096]{1,0:T(4,128)} %param.9) | copy-start | bytes 196612
Sparse Core Ops, SparseCore 0:
  9.1 97.9 all-gather.1
  146.4 83.4 reduce-scatter.1
where the time goes:
time: 254 us; the launch traced here: 252 us
  waiting for transfers between devices  177 us (70%)
  matrix products  31.5 us (12%)
  blocking collectives  13.8 us (5%)
  between operations  13.4 us (5%)
  local copies, waits for them, and re-layouts  9.09 us (4%)
  other arithmetic  7.16 us (3%)
    all_gather x1, waiting for transfers between devices, per_device(): lax.all_gather(amplitudes, 'ab', axis=0, tiled=True)  92.7 us
    reduce_scatter x1, waiting for transfers between devices, per_device(): reduced = lax.psum_scatter(ordered, 'cd', scatter_dimension=0, tiled=True)  83.6 us
    dot_general x1, matrix products, dense_product(): jnp.dot(left_part, right_part * weights[:, None], preferred_element_type=...  31.5 us
    all_to_all x1, blocking collectives, per_device(): lax.all_to_all(reduced.reshape(count_ab, out_rows, columns_dev), 'ab', sp...  13.8 us
    gather x1, other arithmetic, dense_product(): jnp.repeat(live_tiles.astype(jnp.float32), tile_size, total_repeat_length...  5.85 us
  transfers between devices with their start and end apart: 2, of which 2 were waited for; matrix products, arithmetic and copies ran while one was open for 3% of the time, Pallas kernels for 0%

commit v1 on v0

v1 whole, which is shorter than its diff:
```python
import functools

import jax
import jax.numpy as jnp
from jax import lax
from jax.experimental import pallas as pl
from jax.experimental.pallas import tpu as pltpu
from jax.sharding import PartitionSpec as P

TILE = 256
HALF = 256
MESH = pl.DeviceIdType.MESH


def kernel(
    planes,
    chips,
    tiles,
    a_ref,
    b_ref,
    live_ref,
    residual_ref,
    out_ref,
    a_all,
    b_raw,
    b_hi,
    b_lo,
    part,
    pair_recv,
    plane_recv,
    summed,
    land,
    a_sem,
    b_sem,
    up_send,
    up_recv,
    down_send,
    down_recv,
    pair_send,
    pair_got,
    plane_send,
    plane_got,
    row_send,
    row_got,
):
    cd = lax.axis_index("cd")
    z = lax.axis_index("ab")
    chip, core = cd // 2, cd % 2
    twin = cd + 1 - 2 * core
    above, below = (z + 1) % planes, (z + planes - 1) % planes
    middle = planes // 2
    rows = a_ref.shape[0]

    barrier = pltpu.get_barrier_semaphore()

    def greet(cd_at, z_at):
        pl.semaphore_signal(barrier, inc=1, device_id={"cd": cd_at, "ab": z_at}, device_id_type=MESH)

    greet(cd, above)
    greet(cd, below)
    greet(twin, z)
    greet(twin, above)
    greet(twin, below)

    @pl.loop(2, planes - 1)
    def _(d):
        greet(cd, (z + d) % planes)
        greet(twin, (z + d) % planes)

    @pl.loop(1, chips)
    def _(d):
        greet(((chip + d) % chips) * 2 + core, z)

    def own_copy(t):
        return pltpu.make_async_copy(
            a_ref.at[:, pl.ds(pl.multiple_of(t * TILE, TILE), TILE)], a_all.at[0, t], a_sem.at[t]
        )

    def b_copy(t):
        return pltpu.make_async_copy(
            b_ref.at[pl.ds(pl.multiple_of(t * TILE, TILE), TILE), :], b_raw.at[t], b_sem.at[t]
        )

    @pl.loop(0, tiles)
    def _(t):
        own_copy(t).start()
        b_copy(t).start()

    part[...] = jnp.zeros_like(part)
    pl.semaphore_wait(barrier, 2 * (planes - 1) + chips)

    def up_copy(step, t):
        return pltpu.make_async_remote_copy(
            src_ref=a_all.at[step, t],
            dst_ref=a_all.at[step + 1, t],
            send_sem=up_send.at[step, t],
            recv_sem=up_recv.at[step, t],
            device_id={"cd": cd, "ab": above},
            device_id_type=MESH,
        )

    def down_copy(step, t):
        return pltpu.make_async_remote_copy(
            src_ref=a_all.at[(planes - step) % planes, t],
            dst_ref=a_all.at[planes - 1 - step, t],
            send_sem=down_send.at[step, t],
            recv_sem=down_recv.at[step, t],
            device_id={"cd": cd, "ab": below},
            device_id_type=MESH,
        )

    @pl.loop(0, tiles)
    def _(t):
        own_copy(t).wait()

    @pl.loop(0, tiles)
    def _(t):
        up_copy(0, t).start()
        down_copy(0, tiles - 1 - t).start()

    @pl.loop(0, tiles)
    def _(t):
        b_copy(t).wait()
        weight = live_ref[t].astype(jnp.float32)
        whole = b_raw[t] * weight
        high = whole.astype(jnp.bfloat16)
        b_hi[t] = high
        b_lo[t] = (whole - high.astype(jnp.float32)).astype(jnp.bfloat16)

    def multiply(slot, t):
        whole = a_all[slot, t]
        high = whole.astype(jnp.bfloat16)
        low = (whole - high.astype(jnp.float32)).astype(jnp.bfloat16)
        both = jnp.concatenate([high, low], axis=0)
        for h in range(2):
            cols = slice(h * HALF, (h + 1) * HALF)
            first = jnp.dot(both, b_hi[t, :, cols], preferred_element_type=jnp.float32)
            second = jnp.dot(high, b_lo[t, :, cols], preferred_element_type=jnp.float32)
            part[slot, h] += first[:rows] + (first[rows:] + second)

    def pair_copy(slot):
        return pltpu.make_async_remote_copy(
            src_ref=part.at[slot, 1 - core],
            dst_ref=pair_recv.at[slot],
            send_sem=pair_send.at[slot],
            recv_sem=pair_got.at[slot],
            device_id={"cd": twin, "ab": z},
            device_id_type=MESH,
        )

    def plane_copy(slot, d):
        to = (chip + d) % chips
        return pltpu.make_async_remote_copy(
            src_ref=part.at[slot, core, pl.ds(pl.multiple_of(to * 8, 8), 8)],
            dst_ref=plane_recv.at[slot, pl.ds(pl.multiple_of((d - 1) * 8, 8), 8)],
            send_sem=plane_send.at[slot],
            recv_sem=plane_got.at[slot],
            device_id={"cd": to * 2 + core, "ab": z},
            device_id_type=MESH,
        )

    def plane_whole(slot):
        return pltpu.make_async_remote_copy(
            src_ref=part.at[slot, core, pl.ds(0, (chips - 1) * 8)],
            dst_ref=plane_recv.at[slot],
            send_sem=plane_send.at[slot],
            recv_sem=plane_got.at[slot],
            device_id={"cd": twin, "ab": z},
            device_id_type=MESH,
        )

    def row_copy(slot, to_twin):
        return pltpu.make_async_remote_copy(
            src_ref=summed.at[slot],
            dst_ref=land.at[2 * z + core],
            send_sem=row_send.at[slot, to_twin],
            recv_sem=row_got.at[2 * z + core],
            device_id={"cd": twin if to_twin else cd, "ab": (z + planes - slot) % planes},
            device_id_type=MESH,
        )

    def send_pair(slot):
        pair_copy(slot).start()

    def send_plane(slot):
        pair_copy(slot).wait_recv()
        part[slot, core] += pair_recv[slot]

        @pl.loop(1, chips)
        def _(d):
            plane_copy(slot, d).start()

    def send_rows(slot):
        plane_whole(slot).wait_recv()
        mine = part[slot, core, pl.ds(pl.multiple_of(chip * 8, 8), 8)]
        total = mine + jnp.sum(plane_recv[slot].reshape(chips - 1, 8, HALF), axis=0)
        summed[slot] = total
        row_copy(slot, 1).start()
        if isinstance(slot, int) and slot == 0:
            land[2 * z + core] = total
        else:
            row_copy(slot, 0).start()

    @pl.loop(0, tiles)
    def _(t):
        multiply(0, t)

    send_pair(0)
    send_plane(0)

    def ring_step(step, j):
        up_copy(step - 1, j).wait_recv()

        @pl.when(jnp.logical_or(step < middle - 1, j < tiles // 2))
        def _():
            up_copy(step, j).start()

        down_copy(step - 1, tiles - 1 - j).wait_recv()

        @pl.when(jnp.logical_or(step < middle - 1, j < tiles // 2))
        def _():
            down_copy(step, tiles - 1 - j).start()

        multiply(step, j)
        multiply(planes - step, tiles - 1 - j)

    @pl.loop(1, middle)
    def _(step):
        @pl.loop(0, tiles)
        def _(j):
            ring_step(step, j)

            @pl.when(jnp.logical_and(step == 1, j == 2))
            def _():
                send_rows(0)

            @pl.when(jnp.logical_and(step > 1, j == 0))
            def _():
                send_plane(step - 1)
                send_plane(planes - step + 1)

            @pl.when(jnp.logical_and(step > 1, j == 3))
            def _():
                send_rows(step - 1)
                send_rows(planes - step + 1)

        send_pair(step)
        send_pair(planes - step)

    @pl.loop(0, tiles // 2)
    def _(j):
        up_copy(middle - 1, j).wait_recv()
        down_copy(middle - 1, tiles - 1 - j).wait_recv()
        multiply(middle, j)
        multiply(middle, tiles - 1 - j)

        @pl.when(j == 0)
        def _():
            send_plane(middle - 1)
            send_plane(middle + 1)

        @pl.when(j == tiles // 4)
        def _():
            send_rows(middle - 1)
            send_rows(middle + 1)

    send_pair(middle)
    send_plane(middle)
    send_rows(middle)

    @pl.loop(1, 2 * planes)
    def _(d):
        at = (2 * z + core + d) % (2 * planes)
        pltpu.make_async_remote_copy(
            src_ref=summed.at[0],
            dst_ref=land.at[at],
            send_sem=row_send.at[0, 0],
            recv_sem=row_got.at[at],
            device_id={"cd": twin, "ab": z},
            device_id_type=MESH,
        ).wait_recv()

    for at in range(2 * planes):
        cols = slice(at * HALF, (at + 1) * HALF)
        got = land[at]
        out_ref[:, cols] = residual_ref[:, cols] + jnp.where(core == 0, got[:4], got[4:])

    @pl.loop(0, middle)
    def _(step):
        @pl.loop(0, tiles)
        def _(j):
            @pl.when(jnp.logical_or(step < middle - 1, j < tiles // 2))
            def _():
                up_copy(step, j).wait_send()
                down_copy(step, tiles - 1 - j).wait_send()

    @pl.loop(0, planes)
    def _(slot):
        pair_copy(slot).wait_send()
        plane_whole(slot).wait_send()
        row_copy(slot, 1).wait_send()

        @pl.when(slot > 0)
        def _():
            row_copy(slot, 0).wait_send()


def solution(mesh):
    planes, chips = mesh.shape["ab"], mesh.shape["cd"] // 2

    def per_device(amplitudes, integrals, live_tiles, residual_in):
        rows, depth = amplitudes.shape
        tiles, columns = depth // TILE, integrals.shape[1]
        f32, bf16 = jnp.float32, jnp.bfloat16
        dma = pltpu.SemaphoreType.DMA
        return pl.pallas_call(
            functools.partial(kernel, planes, chips, tiles),
            out_shape=jax.ShapeDtypeStruct(residual_in.shape, f32),
            in_specs=[
                pl.BlockSpec(memory_space=pl.ANY),
                pl.BlockSpec(memory_space=pl.ANY),
                pl.BlockSpec(memory_space=pltpu.SMEM),
                pl.BlockSpec(memory_space=pltpu.VMEM),
            ],
            out_specs=pl.BlockSpec(memory_space=pltpu.VMEM),
            scratch_shapes=[
                pltpu.VMEM((planes, tiles, rows, TILE), f32),
                pltpu.VMEM((tiles, TILE, columns), f32),
                pltpu.VMEM((tiles, TILE, columns), bf16),
                pltpu.VMEM((tiles, TILE, columns), bf16),
                pltpu.VMEM((planes, 2, rows, HALF), f32),
                pltpu.VMEM((planes, rows, HALF), f32),
                pltpu.VMEM((planes, (chips - 1) * 8, HALF), f32),
                pltpu.VMEM((planes, 8, HALF), f32),
                pltpu.VMEM((2 * planes, 8, HALF), f32),
                dma((tiles,)),
                dma((tiles,)),
                dma((planes // 2, tiles)),
                dma((planes // 2, tiles)),
                dma((planes // 2, tiles)),
                dma((planes // 2, tiles)),
                dma((planes,)),
                dma((planes,)),
                dma((planes,)),
                dma((planes,)),
                dma((planes, 2)),
                dma((2 * planes,)),
            ],
            compiler_params=pltpu.CompilerParams(
                collective_id=0, has_side_effects=True, vmem_limit_bytes=48 * 1024 * 1024
            ),
            cost_estimate=pl.CostEstimate(
                flops=6 * planes * rows * depth * columns,
                bytes_accessed=4 * depth * (rows + columns),
                transcendentals=0,
            ),
        )(amplitudes, integrals, live_tiles, residual_in)

    return jax.shard_map(
        per_device,
        mesh=mesh,
        in_specs=(P("ab", "cd"), P("cd", "ab"), P("cd"), P(("ab", "cd"), None)),
        out_specs=P(("ab", "cd"), None),
        check_vma=False,
    )
```

time: 254 us -> 112 us (0.44)
  waiting for transfers between devices: 177 us -> 0 us
  Pallas kernels: 0 us -> 106 us
  matrix products: 31.5 us -> 0 us
  blocking collectives: 13.8 us -> 0 us
  between operations: 13.4 us -> 0.01 us
  other arithmetic: 7.16 us -> 0 us
  local copies, waits for them, and re-layouts: 9.09 us -> 5.54 us
    pallas_call x0 -> x1, Pallas kernels: none -> 106 us  [per_device(): pl.pallas_call(functools.partial(kernel, planes, chips, tiles), out_shape...]
    all_gather x1 -> x0, waiting for transfers between devices: 92.7 us -> none  [per_device(): lax.all_gather(amplitudes, 'ab', axis=0, tiled=True)]
    reduce_scatter x1 -> x0, waiting for transfers between devices: 83.6 us -> none  [per_device(): reduced = lax.psum_scatter(ordered, 'cd', scatter_dimension=0, tiled=True)]
    dot_general x1 -> x0, matrix products: 31.5 us -> none  [dense_product(): jnp.dot(left_part, right_part * weights[:, None], preferred_element_type=...]
    all_to_all x1 -> x0, blocking collectives: 13.8 us -> none  [per_device(): lax.all_to_all(reduced.reshape(count_ab, out_rows, columns_dev), 'ab', sp...]
    gather x1 -> x0, other arithmetic: 5.85 us -> none  [dense_product(): jnp.repeat(live_tiles.astype(jnp.float32), tile_size, total_repeat_length...]
    unnamed x2 -> x9, local copies, waits for them, and re-layouts: 0.01 us -> 5.54 us
    reshape x3 -> x0, local copies, waits for them, and re-layouts: 4.3 us -> none  [the longest x1 1.78 us: per_device(): ordered = ordered.reshape(count_cd * count_ab * out_rows, columns_dev)]
  transfers between devices with their start and end apart: 2 -> 0, of which waited for: 2 -> 0; matrix products, arithmetic and copies ran while one was open for 3% -> 0% of each run, Pallas kernels for 0% -> 0%
where the time goes in v1:
time: 112 us
  Pallas kernels  106 us (95%)
  local copies, waits for them, and re-layouts  5.54 us (5%)
    pallas_call x1, Pallas kernels, per_device(): pl.pallas_call(functools.partial(kernel, planes, chips, tiles), out_shape...  106 us
    unnamed x9, local copies, waits for them, and re-layouts  5.54 us

profile of v1, /device:TPU:1, one launch (start us, length us, event | category | flops | bytes accessed | tf_op | source)
XLA Modules:
  0.0 111.6 jit_solution(9658385705176612945)
XLA Ops:
  0.0 0.0 copy-start
  0.0 2.2 %copy-done = f32[2048,512]{1,0:T(8,128)S(1)} copy-done((f32[2048,512]{1,0:T(8,128)S(1)}, f32[2048,512]{1,0:T(8,128)}, u32[]{:S(2)}) %copy-start) | copy-done | bytes 4194328
  2.2 0.0 copy-start.1
  2.2 1.2 %copy-done.1 = f32[128,2048]{1,0:T(8,128)S(1)} copy-done((f32[128,2048]{1,0:T(8,128)S(1)}, f32[128,2048]{1,0:T(8,128)}, u32[]{:S(2)}) %copy-start.1) | copy-done | bytes 1048600
  3.4 0.0 copy-start.2
  3.4 0.8 copy-done.2
  4.3 0.0 copy-start.3
  4.3 0.7 copy-done.3
  4.9 106.0 %shard_map.46 = f32[4,4096]{1,0:T(4,128)S(1)} custom-call(f32[128,2048]{1,0:T(8,128)S(1)} %copy-done.1, f32[2048,512]{1,0:T(8,128)S(1)} %copy-done, s32[8]{0:T(128)S(1)} %copy-done.3, f32[4,4096]{1,0:T(4,128)S(1)} %copy-done.2), custom_call_target="tpu_custom_call" | custom-call | flops 6442450944 | bytes 5242880 | tf_op jit(solution)/shard_map/pallas_call | solution.py:316
  111.0 0.6 copy.6
Async XLA Ops:
  0.0 2.2 %copy-start = (f32[2048,512]{1,0:T(8,128)S(1)}, f32[2048,512]{1,0:T(8,128)}, u32[]{:S(2)}) copy-start(f32[2048,512]{1,0:T(8,128)} %b_ref.1) | copy-start | bytes 12582916
  2.2 1.2 %copy-start.1 = (f32[128,2048]{1,0:T(8,128)S(1)}, f32[128,2048]{1,0:T(8,128)}, u32[]{:S(2)}) copy-start(f32[128,2048]{1,0:T(8,128)} %a_ref.1) | copy-start | bytes 3145732
  3.4 0.8 copy-start.2
  4.3 0.7 copy-start.3

commit v2 on v1

--- a/solution.py
+++ b/solution.py
@@ -19,17 +19,19 @@
     a_ref,
     b_ref,
     live_ref,
-    residual_ref,
     out_ref,
     a_all,
     b_raw,
     b_hi,
     b_lo,
     part,
+    folded,
     pair_recv,
     plane_recv,
     summed,
     land,
+    live,
+    live_sem,
     a_sem,
     b_sem,
     up_send,
@@ -59,39 +61,39 @@
     greet(cd, above)
     greet(cd, below)
     greet(twin, z)
-    greet(twin, above)
-    greet(twin, below)
 
     @pl.loop(2, planes - 1)
     def _(d):
         greet(cd, (z + d) % planes)
-        greet(twin, (z + d) % planes)
 
     @pl.loop(1, chips)
     def _(d):
         greet(((chip + d) % chips) * 2 + core, z)
 
+    def a_tile(t):
+        return a_ref.at[:, pl.ds(pl.multiple_of(t * TILE, TILE), TILE)]
+
     def own_copy(t):
-        return pltpu.make_async_copy(
-            a_ref.at[:, pl.ds(pl.multiple_of(t * TILE, TILE), TILE)], a_all.at[0, t], a_sem.at[t]
-        )
+        return pltpu.make_async_copy(a_tile(t), a_all.at[0, t], a_sem.at[t])
 
     def b_copy(t):
         return pltpu.make_async_copy(
             b_ref.at[pl.ds(pl.multiple_of(t * TILE, TILE), TILE), :], b_raw.at[t], b_sem.at[t]
         )
 
+    live_copy = pltpu.make_async_copy(live_ref, live, live_sem)
+    live_copy.start()
+
     @pl.loop(0, tiles)
     def _(t):
         own_copy(t).start()
         b_copy(t).start()
 
-    part[...] = jnp.zeros_like(part)
-    pl.semaphore_wait(barrier, 2 * (planes - 1) + chips)
-
-    def up_copy(step, t):
-        return pltpu.make_async_remote_copy(
-            src_ref=a_all.at[step, t],
+    pl.semaphore_wait(barrier, planes - 1 + chips)
+
+    def up_copy(step, t, src=None):
+        return pltpu.make_async_remote_copy(
+            src_ref=a_all.at[step, t] if src is None else src,
             dst_ref=a_all.at[step + 1, t],
             send_sem=up_send.at[step, t],
             recv_sem=up_recv.at[step, t],
@@ -99,9 +101,9 @@
             device_id_type=MESH,
         )
 
-    def down_copy(step, t):
-        return pltpu.make_async_remote_copy(
-            src_ref=a_all.at[(planes - step) % planes, t],
+    def down_copy(step, t, src=None):
+        return pltpu.make_async_remote_copy(
+            src_ref=a_all.at[(planes - step) % planes, t] if src is None else src,
             dst_ref=a_all.at[planes - 1 - step, t],
             send_sem=down_send.at[step, t],
             recv_sem=down_recv.at[step, t],
@@ -111,17 +113,17 @@
 
     @pl.loop(0, tiles)
     def _(t):
-        own_copy(t).wait()
-
-    @pl.loop(0, tiles)
-    def _(t):
-        up_copy(0, t).start()
-        down_copy(0, tiles - 1 - t).start()
+        up_copy(0, t, a_tile(t)).start()
+        down_copy(0, tiles - 1 - t, a_tile(tiles - 1 - t)).start()
+
+    part[...] = jnp.zeros_like(part)
+
+    live_copy.wait()
 
     @pl.loop(0, tiles)
     def _(t):
         b_copy(t).wait()
-        weight = live_ref[t].astype(jnp.float32)
+        weight = live[t].astype(jnp.float32)
         whole = b_raw[t] * weight
         high = whole.astype(jnp.bfloat16)
         b_hi[t] = high
@@ -140,7 +142,7 @@
 
     def pair_copy(slot):
         return pltpu.make_async_remote_copy(
-            src_ref=part.at[slot, 1 - core],
+            src_ref=folded.at[slot, 1 - core],
             dst_ref=pair_recv.at[slot],
             send_sem=pair_send.at[slot],
             recv_sem=pair_got.at[slot],
@@ -151,7 +153,7 @@
     def plane_copy(slot, d):
         to = (chip + d) % chips
         return pltpu.make_async_remote_copy(
-            src_ref=part.at[slot, core, pl.ds(pl.multiple_of(to * 8, 8), 8)],
+            src_ref=folded.at[slot, core, pl.ds(pl.multiple_of(to * 8, 8), 8)],
             dst_ref=plane_recv.at[slot, pl.ds(pl.multiple_of((d - 1) * 8, 8), 8)],
             send_sem=plane_send.at[slot],
             recv_sem=plane_got.at[slot],
@@ -161,7 +163,7 @@
 
     def plane_whole(slot):
         return pltpu.make_async_remote_copy(
-            src_ref=part.at[slot, core, pl.ds(0, (chips - 1) * 8)],
+            src_ref=folded.at[slot, core, pl.ds(0, (chips - 1) * 8)],
             dst_ref=plane_recv.at[slot],
             send_sem=plane_send.at[slot],
             recv_sem=plane_got.at[slot],
@@ -169,40 +171,57 @@
             device_id_type=MESH,
         )
 
-    def row_copy(slot, to_twin):
+    def row_copy(slot):
         return pltpu.make_async_remote_copy(
             src_ref=summed.at[slot],
-            dst_ref=land.at[2 * z + core],
-            send_sem=row_send.at[slot, to_twin],
-            recv_sem=row_got.at[2 * z + core],
-            device_id={"cd": twin if to_twin else cd, "ab": (z + planes - slot) % planes},
+            dst_ref=land.at[slot],
+            send_sem=row_send.at[slot],
+            recv_sem=row_got.at[slot],
+            device_id={"cd": cd, "ab": (z + planes - slot) % planes},
             device_id_type=MESH,
         )
 
     def send_pair(slot):
+        left, right = part[slot, 0], part[slot, 1]
+        upper = lax.broadcasted_iota(jnp.int32, left.shape, 0) % 8 < 4
+        folded[slot, 0] = jnp.where(upper, left, pltpu.roll(right, 4, 0))
+        folded[slot, 1] = jnp.where(upper, pltpu.roll(left, rows - 4, 0), right)
         pair_copy(slot).start()
 
     def send_plane(slot):
         pair_copy(slot).wait_recv()
-        part[slot, core] += pair_recv[slot]
+        folded[slot, core] += pair_recv[slot]
 
         @pl.loop(1, chips)
         def _(d):
             plane_copy(slot, d).start()
 
+    def write_rows(slot, got):
+        first = ((z + slot) % planes) * (2 * HALF)
+        for h in range(2):
+            cols = pl.ds(pl.multiple_of(first + h * HALF, HALF), HALF)
+            out_ref[:, cols] = got[4 * h : 4 * h + 4]
+
     def send_rows(slot):
         plane_whole(slot).wait_recv()
-        mine = part[slot, core, pl.ds(pl.multiple_of(chip * 8, 8), 8)]
+        mine = folded[slot, core, pl.ds(pl.multiple_of(chip * 8, 8), 8)]
         total = mine + jnp.sum(plane_recv[slot].reshape(chips - 1, 8, HALF), axis=0)
-        summed[slot] = total
-        row_copy(slot, 1).start()
         if isinstance(slot, int) and slot == 0:
-            land[2 * z + core] = total
+            write_rows(0, total)
         else:
-            row_copy(slot, 0).start()
+            summed[slot] = total
+
+    def take_rows(slot):
+        row_copy(slot).wait_recv()
+        write_rows(slot, land[slot])
+
+    def ring_sent(step, j):
+        up_copy(step, j).wait_send()
+        down_copy(step, tiles - 1 - j).wait_send()
 
     @pl.loop(0, tiles)
     def _(t):
+        own_copy(t).wait()
         multiply(0, t)
 
     send_pair(0)
@@ -223,6 +242,10 @@
 
         multiply(step, j)
         multiply(planes - step, tiles - 1 - j)
+
+        @pl.when(step > 1)
+        def _():
+            ring_sent(step - 2, j)
 
     @pl.loop(1, middle)
     def _(step):
@@ -265,44 +288,41 @@
             send_rows(middle + 1)
 
     send_pair(middle)
+
+    @pl.loop(1, middle)
+    def _(slot):
+        row_copy(slot).start()
+        row_copy(planes - slot).start()
+
     send_plane(middle)
+
+    @pl.loop(0, tiles)
+    def _(j):
+        ring_sent(middle - 2, j)
+
+    @pl.loop(0, tiles // 2)
+    def _(j):
+        ring_sent(middle - 1, j)
+
     send_rows(middle)
-
-    @pl.loop(1, 2 * planes)
-    def _(d):
-        at = (2 * z + core + d) % (2 * planes)
-        pltpu.make_async_remote_copy(
-            src_ref=summed.at[0],
-            dst_ref=land.at[at],
-            send_sem=row_send.at[0, 0],
-            recv_sem=row_got.at[at],
-            device_id={"cd": twin, "ab": z},
-            device_id_type=MESH,
-        ).wait_recv()
-
-    for at in range(2 * planes):
-        cols = slice(at * HALF, (at + 1) * HALF)
-        got = land[at]
-        out_ref[:, cols] = residual_ref[:, cols] + jnp.where(core == 0, got[:4], got[4:])
-
-    @pl.loop(0, middle)
-    def _(step):
-        @pl.loop(0, tiles)
-        def _(j):
-            @pl.when(jnp.logical_or(step < middle - 1, j < tiles // 2))
-            def _():
-                up_copy(step, j).wait_send()
-                down_copy(step, tiles - 1 - j).wait_send()
+    row_copy(middle).start()
+
+    @pl.loop(1, middle)
+    def _(slot):
+        take_rows(slot)
+        take_rows(planes - slot)
 
     @pl.loop(0, planes)
     def _(slot):
         pair_copy(slot).wait_send()
         plane_whole(slot).wait_send()
-        row_copy(slot, 1).wait_send()
-
-        @pl.when(slot > 0)
-        def _():
-            row_copy(slot, 0).wait_send()
+
+        @pl.when(jnp.logical_and(slot > 0, slot != middle))
+        def _():
+            row_copy(slot).wait_send()
+
+    take_rows(middle)
+    row_copy(middle).wait_send()
 
 
 def solution(mesh):
@@ -313,14 +333,13 @@
         tiles, columns = depth // TILE, integrals.shape[1]
         f32, bf16 = jnp.float32, jnp.bfloat16
         dma = pltpu.SemaphoreType.DMA
-        return pl.pallas_call(
+        ladder = pl.pallas_call(
             functools.partial(kernel, planes, chips, tiles),
-            out_shape=jax.ShapeDtypeStruct(residual_in.shape, f32),
+            out_shape=pltpu.VMEM(residual_in.shape, f32),
             in_specs=[
-                pl.BlockSpec(memory_space=pl.ANY),
-                pl.BlockSpec(memory_space=pl.ANY),
-                pl.BlockSpec(memory_space=pltpu.SMEM),
-                pl.BlockSpec(memory_space=pltpu.VMEM),
+                pl.BlockSpec(memory_space=pltpu.HBM),
+                pl.BlockSpec(memory_space=pltpu.HBM),
+                pl.BlockSpec(memory_space=pltpu.HBM),
             ],
             out_specs=pl.BlockSpec(memory_space=pltpu.VMEM),
             scratch_shapes=[
@@ -329,10 +348,13 @@
                 pltpu.VMEM((tiles, TILE, columns), bf16),
                 pltpu.VMEM((tiles, TILE, columns), bf16),
                 pltpu.VMEM((planes, 2, rows, HALF), f32),
+                pltpu.VMEM((planes, 2, rows, HALF), f32),
                 pltpu.VMEM((planes, rows, HALF), f32),
                 pltpu.VMEM((planes, (chips - 1) * 8, HALF), f32),
                 pltpu.VMEM((planes, 8, HALF), f32),
-                pltpu.VMEM((2 * planes, 8, HALF), f32),
+                pltpu.VMEM((planes, 8, HALF), f32),
+                pltpu.SMEM((tiles,), jnp.int32),
+                dma(()),
                 dma((tiles,)),
                 dma((tiles,)),
                 dma((planes // 2, tiles)),
@@ -343,18 +365,19 @@
                 dma((planes,)),
                 dma((planes,)),
                 dma((planes,)),
-                dma((planes, 2)),
-                dma((2 * planes,)),
+                dma((planes,)),
+                dma((planes,)),
             ],
             compiler_params=pltpu.CompilerParams(
-                collective_id=0, has_side_effects=True, vmem_limit_bytes=48 * 1024 * 1024
+                collective_id=0, has_side_effects=True, vmem_limit_bytes=58 * 1024 * 1024
             ),
             cost_estimate=pl.CostEstimate(
                 flops=6 * planes * rows * depth * columns,
                 bytes_accessed=4 * depth * (rows + columns),
                 transcendentals=0,
             ),
-        )(amplitudes, integrals, live_tiles, residual_in)
+        )(amplitudes, integrals, live_tiles)
+        return residual_in + ladder
 
     return jax.shard_map(
         per_device,

time: 112 us -> 104 us (0.929)
  local copies, waits for them, and re-layouts: 5.54 us -> 0.01 us
  Pallas kernels: 106 us -> 103 us
    unnamed x9 -> x2, local copies, waits for them, and re-layouts: 5.54 us -> 0.01 us
    pallas_call x1, Pallas kernels: 106 us -> 103 us  [per_device(): pl.pallas_call(functools.partial(kernel, planes, chips, tiles), out_shape...]
where the time goes in v2:
time: 104 us
  Pallas kernels  103 us (99%)
    pallas_call x1, Pallas kernels, per_device(): pl.pallas_call(functools.partial(kernel, planes, chips, tiles), out_shape...  103 us

profile of v2, /device:TPU:1, one launch (start us, length us, event | category | flops | bytes accessed | tf_op | source)
XLA Modules:
  0.0 103.9 jit_solution(18106521581000384835)
XLA Ops:
  0.0 0.0 copy-start
  0.0 103.2 %shard_map.46 = f32[4,4096]{1,0:T(4,128)S(1)} custom-call(f32[128,2048]{1,0:T(8,128)} %a_ref.1, f32[2048,512]{1,0:T(8,128)} %b_ref.1, s32[8]{0:T(128)} %live_ref.1), custom_call_target="tpu_custom_call" | custom-call | flops 6442450944 | bytes 5242880 | tf_op jit(solution)/shard_map/pallas_call | solution.py:336
  103.2 0.0 copy-done
  103.2 0.6 add.3
Async XLA Ops:
  0.0 103.2 %copy-start = (f32[4,4096]{1,0:T(4,128)S(1)}, f32[4,4096]{1,0:T(4,128)}, u32[]{:S(2)}) copy-start(f32[4,4096]{1,0:T(4,128)} %param.7) | copy-start | bytes 196612

commit v3 on v2

--- a/solution.py
+++ b/solution.py
@@ -1,4 +1,5 @@
 import functools
+import math
 
 import jax
 import jax.numpy as jnp
@@ -15,6 +16,7 @@
 def kernel(
     planes,
     chips,
+    line,
     tiles,
     a_ref,
     b_ref,
@@ -31,6 +33,7 @@
     summed,
     land,
     live,
+    relay,
     live_sem,
     a_sem,
     b_sem,
@@ -50,7 +53,8 @@
     chip, core = cd // 2, cd % 2
     twin = cd + 1 - 2 * core
     above, below = (z + 1) % planes, (z + planes - 1) % planes
-    middle = planes // 2
+    half = tiles // 2
+    last = planes - 1
     rows = a_ref.shape[0]
 
     barrier = pltpu.get_barrier_semaphore()
@@ -62,13 +66,18 @@
     greet(cd, below)
     greet(twin, z)
 
-    @pl.loop(2, planes - 1)
+    across, along = chip // line, chip % line
+
+    def in_row(d):
+        return (across * line + (along + d) % line) * 2 + core
+
+    def in_column(d):
+        return ((across + d) % line * line + along) * 2 + core
+
+    @pl.loop(1, line)
     def _(d):
-        greet(cd, (z + d) % planes)
-
-    @pl.loop(1, chips)
-    def _(d):
-        greet(((chip + d) % chips) * 2 + core, z)
+        greet(in_row(d), z)
+        greet(in_column(d), z)
 
     def a_tile(t):
         return a_ref.at[:, pl.ds(pl.multiple_of(t * TILE, TILE), TILE)]
@@ -81,15 +90,7 @@
             b_ref.at[pl.ds(pl.multiple_of(t * TILE, TILE), TILE), :], b_raw.at[t], b_sem.at[t]
         )
 
-    live_copy = pltpu.make_async_copy(live_ref, live, live_sem)
-    live_copy.start()
-
-    @pl.loop(0, tiles)
-    def _(t):
-        own_copy(t).start()
-        b_copy(t).start()
-
-    pl.semaphore_wait(barrier, planes - 1 + chips)
+    pl.semaphore_wait(barrier, 3 + 2 * (line - 1))
 
     def up_copy(step, t, src=None):
         return pltpu.make_async_remote_copy(
@@ -111,10 +112,24 @@
             device_id_type=MESH,
         )
 
-    @pl.loop(0, tiles)
+    @pl.loop(0, half)
     def _(t):
         up_copy(0, t, a_tile(t)).start()
         down_copy(0, tiles - 1 - t, a_tile(tiles - 1 - t)).start()
+
+    up_copy(0, half, a_tile(half)).start()
+
+    @pl.loop(1, line)
+    def _(d):
+        pl.semaphore_signal(relay, inc=1, device_id={"cd": in_row(d), "ab": z}, device_id_type=MESH)
+
+    live_copy = pltpu.make_async_copy(live_ref, live, live_sem)
+    live_copy.start()
+
+    @pl.loop(0, tiles)
+    def _(t):
+        own_copy(t).start()
+        b_copy(t).start()
 
     part[...] = jnp.zeros_like(part)
 
@@ -215,114 +230,162 @@
         row_copy(slot).wait_recv()
         write_rows(slot, land[slot])
 
+    @pl.loop(0, tiles)
+    def _(t):
+        own_copy(t).wait()
+
+    def forward_up(step, j):
+        up_copy(step - 1, j).wait_recv()
+
+        @pl.when(jnp.logical_or(step < last - 1, jnp.logical_and(step < last, j < half - 1)))
+        def _():
+            up_copy(step, j).start()
+
+    def forward_down(step, j):
+        down_copy(step - 1, tiles - 1 - j).wait_recv()
+
+        @pl.when(jnp.logical_or(step < last - 1, jnp.logical_and(step < last, j < half - 1)))
+        def _():
+            down_copy(step, tiles - 1 - j).start()
+
     def ring_sent(step, j):
         up_copy(step, j).wait_send()
         down_copy(step, tiles - 1 - j).wait_send()
 
-    @pl.loop(0, tiles)
-    def _(t):
-        own_copy(t).wait()
-        multiply(0, t)
-
-    send_pair(0)
-    send_plane(0)
-
-    def ring_step(step, j):
-        up_copy(step - 1, j).wait_recv()
-
-        @pl.when(jnp.logical_or(step < middle - 1, j < tiles // 2))
-        def _():
-            up_copy(step, j).start()
-
-        down_copy(step - 1, tiles - 1 - j).wait_recv()
-
-        @pl.when(jnp.logical_or(step < middle - 1, j < tiles // 2))
-        def _():
-            down_copy(step, tiles - 1 - j).start()
-
-        multiply(step, j)
-        multiply(planes - step, tiles - 1 - j)
-
-        @pl.when(step > 1)
-        def _():
-            ring_sent(step - 2, j)
-
-    @pl.loop(1, middle)
+    def plane_sent(slot):
+        pair_copy(slot).wait_send()
+        plane_whole(slot).wait_send()
+
+    @pl.loop(1, last)
     def _(step):
-        @pl.loop(0, tiles)
+        @pl.loop(0, half)
         def _(j):
-            ring_step(step, j)
+            forward_up(step, j)
+            forward_down(step, j)
+            multiply(step, j)
+            multiply(planes - step, tiles - 1 - j)
+
+            @pl.when(step == 1)
+            def _():
+                multiply(0, j)
+                multiply(0, tiles - 1 - j)
+
+            @pl.when(step > 1)
+            def _():
+                ring_sent(step - 2, j)
 
             @pl.when(jnp.logical_and(step == 1, j == 2))
             def _():
+                up_copy(0, half).wait_recv()
+                multiply(1, half)
+
+            @pl.when(jnp.logical_and(step == 2, j == 0))
+            def _():
+                pl.semaphore_wait(relay, line - 1)
+                send_plane(0)
+
+            @pl.when(jnp.logical_and(step == 2, j == 2))
+            def _():
                 send_rows(0)
-
-            @pl.when(jnp.logical_and(step > 1, j == 0))
+                plane_sent(0)
+
+            @pl.when(jnp.logical_and(step == planes // 2 + 1, j == 0))
+            def _():
+                send_plane(planes // 2)
+
+            @pl.when(jnp.logical_and(step == planes // 2 + 1, j == 2))
+            def _():
+                send_rows(planes // 2)
+                plane_sent(planes // 2)
+
+            @pl.when(jnp.logical_and(step > planes // 2 + 1, j == 0))
             def _():
                 send_plane(step - 1)
                 send_plane(planes - step + 1)
 
-            @pl.when(jnp.logical_and(step > 1, j == 3))
+            @pl.when(jnp.logical_and(step > planes // 2 + 1, j == 2))
             def _():
                 send_rows(step - 1)
                 send_rows(planes - step + 1)
-
-        send_pair(step)
-        send_pair(planes - step)
-
-    @pl.loop(0, tiles // 2)
+                plane_sent(step - 1)
+                plane_sent(planes - step + 1)
+
+        @pl.when(step == 1)
+        def _():
+            send_pair(0)
+
+        @pl.when(step == planes // 2)
+        def _():
+            send_pair(planes // 2)
+
+        @pl.when(step > planes // 2)
+        def _():
+            send_pair(step)
+            send_pair(planes - step)
+
+    down_copy(0, half - 1, a_tile(half - 1)).start()
+
+    @pl.loop(0, half - 1)
     def _(j):
-        up_copy(middle - 1, j).wait_recv()
-        down_copy(middle - 1, tiles - 1 - j).wait_recv()
-        multiply(middle, j)
-        multiply(middle, tiles - 1 - j)
+        down_copy(last - 1, tiles - 1 - j).wait_recv()
+        multiply(1, tiles - 1 - j)
+
+        @pl.when(j > 0)
+        def _():
+            up_copy(last - 1, j - 1).wait_recv()
+            multiply(last, j - 1)
 
         @pl.when(j == 0)
         def _():
-            send_plane(middle - 1)
-            send_plane(middle + 1)
-
-        @pl.when(j == tiles // 4)
-        def _():
-            send_rows(middle - 1)
-            send_rows(middle + 1)
-
-    send_pair(middle)
-
-    @pl.loop(1, middle)
+            send_plane(last - 1)
+            send_plane(2)
+
+        @pl.when(j == half - 2)
+        def _():
+            send_pair(1)
+
+    send_rows(last - 1)
+    send_rows(2)
+    plane_sent(last - 1)
+    plane_sent(2)
+    send_plane(1)
+    up_copy(last - 1, half - 2).wait_recv()
+    multiply(last, half - 2)
+    down_copy(0, half - 1).wait_recv()
+    multiply(last, half - 1)
+    send_pair(last)
+
+    @pl.loop(2, last)
     def _(slot):
         row_copy(slot).start()
-        row_copy(planes - slot).start()
-
-    send_plane(middle)
-
-    @pl.loop(0, tiles)
+
+    send_plane(last)
+    send_rows(1)
+    row_copy(1).start()
+
+    @pl.loop(0, half)
     def _(j):
-        ring_sent(middle - 2, j)
-
-    @pl.loop(0, tiles // 2)
+        ring_sent(last - 2, j)
+
+    send_rows(last)
+    row_copy(last).start()
+
+    @pl.loop(0, half - 1)
     def _(j):
-        ring_sent(middle - 1, j)
-
-    send_rows(middle)
-    row_copy(middle).start()
-
-    @pl.loop(1, middle)
+        ring_sent(last - 1, j)
+
+    up_copy(0, half).wait_send()
+    down_copy(0, half - 1).wait_send()
+    plane_sent(1)
+    plane_sent(last)
+
+    @pl.loop(1, last)
     def _(slot):
         take_rows(slot)
-        take_rows(planes - slot)
-
-    @pl.loop(0, planes)
-    def _(slot):
-        pair_copy(slot).wait_send()
-        plane_whole(slot).wait_send()
-
-        @pl.when(jnp.logical_and(slot > 0, slot != middle))
-        def _():
-            row_copy(slot).wait_send()
-
-    take_rows(middle)
-    row_copy(middle).wait_send()
+        row_copy(slot).wait_send()
+
+    take_rows(last)
+    row_copy(last).wait_send()
 
 
 def solution(mesh):
@@ -334,7 +397,7 @@
         f32, bf16 = jnp.float32, jnp.bfloat16
         dma = pltpu.SemaphoreType.DMA
         ladder = pl.pallas_call(
-            functools.partial(kernel, planes, chips, tiles),
+            functools.partial(kernel, planes, chips, math.isqrt(chips), tiles),
             out_shape=pltpu.VMEM(residual_in.shape, f32),
             in_specs=[
                 pl.BlockSpec(memory_space=pltpu.HBM),
@@ -354,13 +417,14 @@
                 pltpu.VMEM((planes, 8, HALF), f32),
                 pltpu.VMEM((planes, 8, HALF), f32),
                 pltpu.SMEM((tiles,), jnp.int32),
+                pltpu.SemaphoreType.REGULAR,
                 dma(()),
                 dma((tiles,)),
                 dma((tiles,)),
-                dma((planes // 2, tiles)),
-                dma((planes // 2, tiles)),
-                dma((planes // 2, tiles)),
-                dma((planes // 2, tiles)),
+                dma((planes - 1, tiles)),
+                dma((planes - 1, tiles)),
+                dma((planes - 1, tiles)),
+                dma((planes - 1, tiles)),
                 dma((planes,)),
                 dma((planes,)),
                 dma((planes,)),

time: 104 us -> 102 us (0.981)
  Pallas kernels: 103 us -> 101 us
    pallas_call x1, Pallas kernels: 103 us -> 101 us  [per_device(): pl.pallas_call(functools.partial(kernel, planes, chips, math.isqrt(chips)...]
where the time goes in v3:
time: 102 us
  Pallas kernels  101 us (99%)
    pallas_call x1, Pallas kernels, per_device(): pl.pallas_call(functools.partial(kernel, planes, chips, math.isqrt(chips)...  101 us

profile of v3, /device:TPU:1, one launch (start us, length us, event | category | flops | bytes accessed | tf_op | source)
XLA Modules:
  0.0 101.8 jit_solution(4304566852028349641)
XLA Ops:
  0.0 0.0 copy-start
  0.0 101.1 %shard_map.46 = f32[4,4096]{1,0:T(4,128)S(1)} custom-call(f32[128,2048]{1,0:T(8,128)} %a_ref.1, f32[2048,512]{1,0:T(8,128)} %b_ref.1, s32[8]{0:T(128)} %live_ref.1), custom_call_target="tpu_custom_call" | custom-call | flops 6442450944 | bytes 5242880 | tf_op jit(solution)/shard_map/pallas_call | solution.py:399
  101.2 0.0 copy-done
  101.2 0.6 add.3
Async XLA Ops:
  0.0 101.2 %copy-start = (f32[4,4096]{1,0:T(4,128)S(1)}, f32[4,4096]{1,0:T(4,128)}, u32[]{:S(2)}) copy-start(f32[4,4096]{1,0:T(4,128)} %param.7) | copy-start | bytes 196612

commit v4 on v3

--- a/solution.py
+++ b/solution.py
@@ -32,6 +32,7 @@
     plane_recv,
     summed,
     land,
+    direct,
     live,
     relay,
     live_sem,
@@ -47,6 +48,8 @@
     plane_got,
     row_send,
     row_got,
+    direct_send,
+    direct_got,
 ):
     cd = lax.axis_index("cd")
     z = lax.axis_index("ab")
@@ -196,6 +199,43 @@
             device_id_type=MESH,
         )
 
+    away = sorted(
+        ((dx, dy) for dx in range(line) for dy in range(line)),
+        key=lambda d: -min(d[0], line - d[0]) - min(d[1], line - d[1]),
+    )
+
+    def direct_copy(at):
+        dx, dy = away[at]
+        to = (across + dx) % line * line + (along + dy) % line
+        return pltpu.make_async_remote_copy(
+            src_ref=folded.at[last, core, pl.ds(pl.multiple_of(to * 8, 8), 8)],
+            dst_ref=direct.at[pl.ds(at * 8, 8)],
+            send_sem=direct_send,
+            recv_sem=direct_got,
+            device_id={"cd": to * 2 + core, "ab": above},
+            device_id_type=MESH,
+        )
+
+    def direct_whole():
+        return pltpu.make_async_remote_copy(
+            src_ref=folded.at[last, core],
+            dst_ref=direct,
+            send_sem=direct_send,
+            recv_sem=direct_got,
+            device_id={"cd": cd, "ab": above},
+            device_id_type=MESH,
+        )
+
+    def send_direct():
+        pair_copy(last).wait_recv()
+        folded[last, core] += pair_recv[last]
+        for at in range(chips):
+            direct_copy(at).start()
+
+    def take_direct():
+        direct_whole().wait_recv()
+        write_rows(last, jnp.sum(direct[...].reshape(chips, 8, HALF), axis=0))
+
     def send_pair(slot):
         left, right = part[slot, 0], part[slot, 1]
         upper = lax.broadcasted_iota(jnp.int32, left.shape, 0) % 8 < 4
@@ -349,17 +389,16 @@
     plane_sent(last - 1)
     plane_sent(2)
     send_plane(1)
+    for slot in sorted(range(2, last), key=lambda d: abs(planes // 2 - d)):
+        row_copy(slot).start()
+
     up_copy(last - 1, half - 2).wait_recv()
     multiply(last, half - 2)
     down_copy(0, half - 1).wait_recv()
     multiply(last, half - 1)
     send_pair(last)
 
-    @pl.loop(2, last)
-    def _(slot):
-        row_copy(slot).start()
-
-    send_plane(last)
+    send_direct()
     send_rows(1)
     row_copy(1).start()
 
@@ -367,9 +406,6 @@
     def _(j):
         ring_sent(last - 2, j)
 
-    send_rows(last)
-    row_copy(last).start()
-
     @pl.loop(0, half - 1)
     def _(j):
         ring_sent(last - 1, j)
@@ -377,15 +413,15 @@
     up_copy(0, half).wait_send()
     down_copy(0, half - 1).wait_send()
     plane_sent(1)
-    plane_sent(last)
+    pair_copy(last).wait_send()
 
     @pl.loop(1, last)
     def _(slot):
         take_rows(slot)
         row_copy(slot).wait_send()
 
-    take_rows(last)
-    row_copy(last).wait_send()
+    take_direct()
+    direct_whole().wait_send()
 
 
 def solution(mesh):
@@ -416,6 +452,7 @@
                 pltpu.VMEM((planes, (chips - 1) * 8, HALF), f32),
                 pltpu.VMEM((planes, 8, HALF), f32),
                 pltpu.VMEM((planes, 8, HALF), f32),
+                pltpu.VMEM((chips * 8, HALF), f32),
                 pltpu.SMEM((tiles,), jnp.int32),
                 pltpu.SemaphoreType.REGULAR,
                 dma(()),
@@ -431,6 +468,8 @@
                 dma((planes,)),
                 dma((planes,)),
                 dma((planes,)),
+                dma(()),
+                dma(()),
             ],
             compiler_params=pltpu.CompilerParams(
                 collective_id=0, has_side_effects=True, vmem_limit_bytes=58 * 1024 * 1024

time: 102 us -> 102 us (level)
  no operation moved by 1% of the time
where the time goes in v4:
time: 102 us
  Pallas kernels  101 us (99%)
    pallas_call x1, Pallas kernels, per_device(): pl.pallas_call(functools.partial(kernel, planes, chips, math.isqrt(chips)...  101 us

profile of v4, /device:TPU:1, one launch (start us, length us, event | category | flops | bytes accessed | tf_op | source)
XLA Modules:
  0.0 101.5 jit_solution(14978980165407884697)
XLA Ops:
  0.0 0.0 copy-start
  0.0 100.8 %shard_map.46 = f32[4,4096]{1,0:T(4,128)S(1)} custom-call(f32[128,2048]{1,0:T(8,128)} %a_ref.1, f32[2048,512]{1,0:T(8,128)} %b_ref.1, s32[8]{0:T(128)} %live_ref.1), custom_call_target="tpu_custom_call" | custom-call | flops 6442450944 | bytes 5242880 | tf_op jit(solution)/shard_map/pallas_call | solution.py:435
  100.8 0.0 copy-done
  100.9 0.6 add.3
Async XLA Ops:
  0.0 100.8 %copy-start = (f32[4,4096]{1,0:T(4,128)S(1)}, f32[4,4096]{1,0:T(4,128)}, u32[]{:S(2)}) copy-start(f32[4,4096]{1,0:T(4,128)} %param.7) | copy-start | bytes 196612

commit v5 on v4

--- a/solution.py
+++ b/solution.py
@@ -52,7 +52,7 @@
     direct_got,
 ):
     cd = lax.axis_index("cd")
-    z = lax.axis_index("ab")
+    z = planes - 1 - lax.axis_index("ab")
     chip, core = cd // 2, cd % 2
     twin = cd + 1 - 2 * core
     above, below = (z + 1) % planes, (z + planes - 1) % planes
@@ -63,7 +63,7 @@
     barrier = pltpu.get_barrier_semaphore()
 
     def greet(cd_at, z_at):
-        pl.semaphore_signal(barrier, inc=1, device_id={"cd": cd_at, "ab": z_at}, device_id_type=MESH)
+        pl.semaphore_signal(barrier, inc=1, device_id={"cd": cd_at, "ab": planes - 1 - z_at}, device_id_type=MESH)
 
     greet(cd, above)
     greet(cd, below)
@@ -101,7 +101,7 @@
             dst_ref=a_all.at[step + 1, t],
             send_sem=up_send.at[step, t],
             recv_sem=up_recv.at[step, t],
-            device_id={"cd": cd, "ab": above},
+            device_id={"cd": cd, "ab": planes - 1 - above},
             device_id_type=MESH,
         )
 
@@ -111,7 +111,7 @@
             dst_ref=a_all.at[planes - 1 - step, t],
             send_sem=down_send.at[step, t],
             recv_sem=down_recv.at[step, t],
-            device_id={"cd": cd, "ab": below},
+            device_id={"cd": cd, "ab": planes - 1 - below},
             device_id_type=MESH,
         )
 
@@ -124,7 +124,7 @@
 
     @pl.loop(1, line)
     def _(d):
-        pl.semaphore_signal(relay, inc=1, device_id={"cd": in_row(d), "ab": z}, device_id_type=MESH)
+        pl.semaphore_signal(relay, inc=1, device_id={"cd": in_row(d), "ab": planes - 1 - z}, device_id_type=MESH)
 
     live_copy = pltpu.make_async_copy(live_ref, live, live_sem)
     live_copy.start()
@@ -164,7 +164,7 @@
             dst_ref=pair_recv.at[slot],
             send_sem=pair_send.at[slot],
             recv_sem=pair_got.at[slot],
-            device_id={"cd": twin, "ab": z},
+            device_id={"cd": twin, "ab": planes - 1 - z},
             device_id_type=MESH,
         )
 
@@ -175,7 +175,7 @@
             dst_ref=plane_recv.at[slot, pl.ds(pl.multiple_of((d - 1) * 8, 8), 8)],
             send_sem=plane_send.at[slot],
             recv_sem=plane_got.at[slot],
-            device_id={"cd": to * 2 + core, "ab": z},
+            device_id={"cd": to * 2 + core, "ab": planes - 1 - z},
             device_id_type=MESH,
         )
 
@@ -185,7 +185,7 @@
             dst_ref=plane_recv.at[slot],
             send_sem=plane_send.at[slot],
             recv_sem=plane_got.at[slot],
-            device_id={"cd": twin, "ab": z},
+            device_id={"cd": twin, "ab": planes - 1 - z},
             device_id_type=MESH,
         )
 
@@ -195,7 +195,7 @@
             dst_ref=land.at[slot],
             send_sem=row_send.at[slot],
             recv_sem=row_got.at[slot],
-            device_id={"cd": cd, "ab": (z + planes - slot) % planes},
+            device_id={"cd": cd, "ab": planes - 1 - (z + planes - slot) % planes},
             device_id_type=MESH,
         )
 
@@ -212,7 +212,7 @@
             dst_ref=direct.at[pl.ds(at * 8, 8)],
             send_sem=direct_send,
             recv_sem=direct_got,
-            device_id={"cd": to * 2 + core, "ab": above},
+            device_id={"cd": to * 2 + core, "ab": planes - 1 - above},
             device_id_type=MESH,
         )
 
@@ -222,7 +222,7 @@
             dst_ref=direct,
             send_sem=direct_send,
             recv_sem=direct_got,
-            device_id={"cd": cd, "ab": above},
+            device_id={"cd": cd, "ab": planes - 1 - above},
             device_id_type=MESH,
         )
 
@@ -252,7 +252,7 @@
             plane_copy(slot, d).start()
 
     def write_rows(slot, got):
-        first = ((z + slot) % planes) * (2 * HALF)
+        first = (planes - 1 - (z + slot) % planes) * (2 * HALF)
         for h in range(2):
             cols = pl.ds(pl.multiple_of(first + h * HALF, HALF), HALF)
             out_ref[:, cols] = got[4 * h : 4 * h + 4]

time: 102 us -> 101 us (level)
  no operation moved by 1% of the time
where the time goes in v5:
time: 101 us
  Pallas kernels  100 us (99%)
    pallas_call x1, Pallas kernels, per_device(): pl.pallas_call(functools.partial(kernel, planes, chips, math.isqrt(chips)...  100 us

profile of v5, /device:TPU:1, one launch (start us, length us, event | category | flops | bytes accessed | tf_op | source)
XLA Modules:
  0.0 100.9 jit_solution(1144828569165525262)
XLA Ops:
  0.0 0.0 copy-start
  0.0 100.2 %shard_map.46 = f32[4,4096]{1,0:T(4,128)S(1)} custom-call(f32[128,2048]{1,0:T(8,128)} %a_ref.1, f32[2048,512]{1,0:T(8,128)} %b_ref.1, s32[8]{0:T(128)} %live_ref.1), custom_call_target="tpu_custom_call" | custom-call | flops 6442450944 | bytes 5242880 | tf_op jit(solution)/shard_map/pallas_call | solution.py:435
  100.2 0.0 copy-done
  100.2 0.6 add.3
Async XLA Ops:
  0.0 100.2 %copy-start = (f32[4,4096]{1,0:T(4,128)S(1)}, f32[4,4096]{1,0:T(4,128)}, u32[]{:S(2)}) copy-start(f32[4,4096]{1,0:T(4,128)} %param.7) | copy-start | bytes 196612

commit v6 on v5

--- a/solution.py
+++ b/solution.py
@@ -204,37 +204,38 @@
         key=lambda d: -min(d[0], line - d[0]) - min(d[1], line - d[1]),
     )
 
-    def direct_copy(at):
+    def direct_copy(way, at):
         dx, dy = away[at]
         to = (across + dx) % line * line + (along + dy) % line
         return pltpu.make_async_remote_copy(
-            src_ref=folded.at[last, core, pl.ds(pl.multiple_of(to * 8, 8), 8)],
-            dst_ref=direct.at[pl.ds(at * 8, 8)],
-            send_sem=direct_send,
-            recv_sem=direct_got,
-            device_id={"cd": to * 2 + core, "ab": planes - 1 - above},
-            device_id_type=MESH,
-        )
-
-    def direct_whole():
-        return pltpu.make_async_remote_copy(
-            src_ref=folded.at[last, core],
-            dst_ref=direct,
-            send_sem=direct_send,
-            recv_sem=direct_got,
-            device_id={"cd": cd, "ab": planes - 1 - above},
-            device_id_type=MESH,
-        )
-
-    def send_direct():
-        pair_copy(last).wait_recv()
-        folded[last, core] += pair_recv[last]
+            src_ref=folded.at[(last, 1)[way], core, pl.ds(pl.multiple_of(to * 8, 8), 8)],
+            dst_ref=direct.at[way, pl.ds(at * 8, 8)],
+            send_sem=direct_send.at[way],
+            recv_sem=direct_got.at[way],
+            device_id={"cd": to * 2 + core, "ab": planes - 1 - (above, below)[way]},
+            device_id_type=MESH,
+        )
+
+    def direct_whole(way):
+        return pltpu.make_async_remote_copy(
+            src_ref=folded.at[(last, 1)[way], core],
+            dst_ref=direct.at[way],
+            send_sem=direct_send.at[way],
+            recv_sem=direct_got.at[way],
+            device_id={"cd": cd, "ab": planes - 1 - (above, below)[way]},
+            device_id_type=MESH,
+        )
+
+    def send_direct(way):
+        slot = (last, 1)[way]
+        pair_copy(slot).wait_recv()
+        folded[slot, core] += pair_recv[slot]
         for at in range(chips):
-            direct_copy(at).start()
-
-    def take_direct():
-        direct_whole().wait_recv()
-        write_rows(last, jnp.sum(direct[...].reshape(chips, 8, HALF), axis=0))
+            direct_copy(way, at).start()
+
+    def take_direct(way):
+        direct_whole(way).wait_recv()
+        write_rows((last, 1)[way], jnp.sum(direct[way].reshape(chips, 8, HALF), axis=0))
 
     def send_pair(slot):
         left, right = part[slot, 0], part[slot, 1]
@@ -386,9 +387,9 @@
 
     send_rows(last - 1)
     send_rows(2)
+    send_direct(1)
     plane_sent(last - 1)
     plane_sent(2)
-    send_plane(1)
     for slot in sorted(range(2, last), key=lambda d: abs(planes // 2 - d)):
         row_copy(slot).start()
 
@@ -398,9 +399,7 @@
     multiply(last, half - 1)
     send_pair(last)
 
-    send_direct()
-    send_rows(1)
-    row_copy(1).start()
+    send_direct(0)
 
     @pl.loop(0, half)
     def _(j):
@@ -412,16 +411,19 @@
 
     up_copy(0, half).wait_send()
     down_copy(0, half - 1).wait_send()
-    plane_sent(1)
+    pair_copy(1).wait_send()
     pair_copy(last).wait_send()
 
-    @pl.loop(1, last)
+    take_direct(1)
+
+    @pl.loop(2, last)
     def _(slot):
         take_rows(slot)
         row_copy(slot).wait_send()
 
-    take_direct()
-    direct_whole().wait_send()
+    take_direct(0)
+    direct_whole(1).wait_send()
+    direct_whole(0).wait_send()
 
 
 def solution(mesh):
@@ -452,7 +454,7 @@
                 pltpu.VMEM((planes, (chips - 1) * 8, HALF), f32),
                 pltpu.VMEM((planes, 8, HALF), f32),
                 pltpu.VMEM((planes, 8, HALF), f32),
-                pltpu.VMEM((chips * 8, HALF), f32),
+                pltpu.VMEM((2, chips * 8, HALF), f32),
                 pltpu.SMEM((tiles,), jnp.int32),
                 pltpu.SemaphoreType.REGULAR,
                 dma(()),
@@ -468,8 +470,8 @@
                 dma((planes,)),
                 dma((planes,)),
                 dma((planes,)),
-                dma(()),
-                dma(()),
+                dma((2,)),
+                dma((2,)),
             ],
             compiler_params=pltpu.CompilerParams(
                 collective_id=0, has_side_effects=True, vmem_limit_bytes=58 * 1024 * 1024

time: 101 us -> 100 us (0.990)
  no operation moved by 1% of the time
where the time goes in v6:
time: 100 us
  Pallas kernels  99.5 us (100%)
    pallas_call x1, Pallas kernels, per_device(): pl.pallas_call(functools.partial(kernel, planes, chips, math.isqrt(chips)...  99.5 us

profile of v6, /device:TPU:1, one launch (start us, length us, event | category | flops | bytes accessed | tf_op | source)
XLA Modules:
  0.0 100.2 jit_solution(12340474211091540947)
XLA Ops:
  0.0 0.0 copy-start
  0.0 99.5 %shard_map.46 = f32[4,4096]{1,0:T(4,128)S(1)} custom-call(f32[128,2048]{1,0:T(8,128)} %a_ref.1, f32[2048,512]{1,0:T(8,128)} %b_ref.1, s32[8]{0:T(128)} %live_ref.1), custom_call_target="tpu_custom_call" | custom-call | flops 6442450944 | bytes 5242880 | tf_op jit(solution)/shard_map/pallas_call | solution.py:437
  99.5 0.0 copy-done
  99.6 0.6 add.3
Async XLA Ops:
  0.0 99.5 %copy-start = (f32[4,4096]{1,0:T(4,128)S(1)}, f32[4,4096]{1,0:T(4,128)}, u32[]{:S(2)}) copy-start(f32[4,4096]{1,0:T(4,128)} %param.7) | copy-start | bytes 196612

commit v7 on v6

--- a/solution.py
+++ b/solution.py
@@ -385,9 +385,9 @@
         def _():
             send_pair(1)
 
+    send_direct(1)
     send_rows(last - 1)
     send_rows(2)
-    send_direct(1)
     plane_sent(last - 1)
     plane_sent(2)
     for slot in sorted(range(2, last), key=lambda d: abs(planes // 2 - d)):

time: 100 us -> 99.6 us (level)
  no operation moved by 1% of the time
where the time goes in v7:
time: 99.6 us
  Pallas kernels  98.9 us (99%)
    pallas_call x1, Pallas kernels, per_device(): pl.pallas_call(functools.partial(kernel, planes, chips, math.isqrt(chips)...  98.9 us

profile of v7, /device:TPU:1, one launch (start us, length us, event | category | flops | bytes accessed | tf_op | source)
XLA Modules:
  0.0 99.6 jit_solution(11625853244342546144)
XLA Ops:
  0.0 0.0 copy-start
  0.0 98.9 %shard_map.46 = f32[4,4096]{1,0:T(4,128)S(1)} custom-call(f32[128,2048]{1,0:T(8,128)} %a_ref.1, f32[2048,512]{1,0:T(8,128)} %b_ref.1, s32[8]{0:T(128)} %live_ref.1), custom_call_target="tpu_custom_call" | custom-call | flops 6442450944 | bytes 5242880 | tf_op jit(solution)/shard_map/pallas_call | solution.py:437
  98.9 0.0 copy-done
  98.9 0.6 add.3
Async XLA Ops:
  0.0 98.9 %copy-start = (f32[4,4096]{1,0:T(4,128)S(1)}, f32[4,4096]{1,0:T(4,128)}, u32[]{:S(2)}) copy-start(f32[4,4096]{1,0:T(4,128)} %param.7) | copy-start | bytes 196612

commit v8 on v7

--- a/solution.py
+++ b/solution.py
@@ -371,6 +371,10 @@
         down_copy(last - 1, tiles - 1 - j).wait_recv()
         multiply(1, tiles - 1 - j)
 
+        @pl.when(j == half - 2)
+        def _():
+            send_pair(1)
+
         @pl.when(j > 0)
         def _():
             up_copy(last - 1, j - 1).wait_recv()
@@ -380,10 +384,6 @@
         def _():
             send_plane(last - 1)
             send_plane(2)
-
-        @pl.when(j == half - 2)
-        def _():
-            send_pair(1)
 
     send_direct(1)
     send_rows(last - 1)

time: 99.6 us -> 99.7 us (level)
  no operation moved by 1% of the time
where the time goes in v8:
time: 99.7 us; the launch traced here: 99.6 us
  Pallas kernels  99 us (99%)
    pallas_call x1, Pallas kernels, per_device(): pl.pallas_call(functools.partial(kernel, planes, chips, math.isqrt(chips)...  99 us

profile of v8, /device:TPU:1, one launch (start us, length us, event | category | flops | bytes accessed | tf_op | source)
XLA Modules:
  0.0 99.6 jit_solution(8026176385026652008)
XLA Ops:
  0.0 0.0 copy-start
  0.0 99.0 %shard_map.46 = f32[4,4096]{1,0:T(4,128)S(1)} custom-call(f32[128,2048]{1,0:T(8,128)} %a_ref.1, f32[2048,512]{1,0:T(8,128)} %b_ref.1, s32[8]{0:T(128)} %live_ref.1), custom_call_target="tpu_custom_call" | custom-call | flops 6442450944 | bytes 5242880 | tf_op jit(solution)/shard_map/pallas_call | solution.py:437
  99.0 0.0 copy-done
  99.0 0.6 add.3
Async XLA Ops:
  0.0 99.0 %copy-start = (f32[4,4096]{1,0:T(4,128)S(1)}, f32[4,4096]{1,0:T(4,128)}, u32[]{:S(2)}) copy-start(f32[4,4096]{1,0:T(4,128)} %param.7) | copy-start | bytes 196612
